TPU v7x, 32 devices: a whole 2x2x4 slice. The times are simulated.
32 devices in a mesh: grp: 2 (over y), row: 4 (over z), col: 2 (over x), hd: 2 (over core).
Axes of the slice: x: 2, y: 2, z: 4, core: 2. Of those that a mesh axis runs over, the one named last changes fastest.
Arguments:
- queries: bfloat16 [8, 64, 32, 1536], P('grp', 'row', 'col', 'hd'), parts along dimension 0, may hold values from -6 to 6
- keys: bfloat16 [8, 64, 32, 1536], P('grp', 'row', 'col', 'hd'), parts along dimension 0, may hold values from -6 to 6
- values: bfloat16 [8, 64, 32, 1536], P('grp', 'row', 'col', 'hd'), parts along dimension 0, may hold values from -6 to 6
- labels: int32 [8, 4, 2], P('grp'), parts along dimension 0, may hold values from 0 to 2
- pad_rows: int32 [2], P('grp'), parts along dimension 0, may hold values from 0 to 31
- pad_cols: int32 [2], P('grp'), parts along dimension 0, may hold values from 0 to 31
Outputs:
- attended: bfloat16 [8, 64, 32, 1536], P('grp', 'row', 'col', 'hd'), parts along dimension 0
There are 2 independent parts, one for each index of `grp`. A program takes and returns all parts, laid end to end along the dimension named above; each array names one. Nothing has to cross between parts.
All inputs are finite; a program needn't handle non-finite values.
Results may differ from a plain program's by a relative error of at most 0.008.
Values may be sent and summed in bfloat16 or wider, within the bound.
A program may use at most 128 MiB of HBM per device.

v0:
```python
import jax
import jax.numpy as jnp
from jax import lax
from jax.sharding import PartitionSpec as P

HDIM = 128


def passed_along(value, axis, by):
    devices = lax.axis_size(axis)
    return lax.ppermute(value, axis, [(i, (i + by) % devices) for i in range(devices)])


def partner_2(value, axis, apart):
    return lax.ppermute(value, axis, [(i, i ^ 1 << apart) for i in range(lax.axis_size(axis))])


def join_partner(source, partner, axis_dim, odd_flag):
    with_upper = jnp.concatenate((source, partner), axis=axis_dim)
    with_lower = jnp.concatenate((partner, source), axis=axis_dim)
    return jnp.where(odd_flag == 1, with_upper, with_lower)


def tile_labels(labels, row_tiles, col_tiles):
    row_match = (
        jnp.arange(labels.shape[1], dtype=jnp.int32)[None, :] == row_tiles[:, None]
    ).astype(jnp.int32)
    col_match = (
        jnp.arange(labels.shape[2], dtype=jnp.int32)[None, :] == col_tiles[:, None]
    ).astype(jnp.int32)
    by_row = jnp.sum(labels[:, None, :, :] * row_match[None, :, :, None], axis=2)
    return jnp.sum(by_row[:, :, None, :] * col_match[None, None, :, :], axis=3)


def per_device(queries, keys, values, labels, pad_rows, pad_cols):
    frames, half_size, tile_cols, channels = queries.shape
    row_count = lax.axis_size("row")
    col_count = lax.axis_size("col")
    row_id = lax.axis_index("row")
    col_id = lax.axis_index("col")
    row_odd = row_id % 2
    col_odd = col_id % 2
    stacked = jnp.stack((keys, values))
    moved = passed_along(stacked, "col", 1)
    moved = partner_2(moved, "col", 0)
    moved = passed_along(moved, "col", -1)
    col_pair = join_partner(stacked, moved, 3, col_odd)
    moved = passed_along(col_pair, "row", 1)
    moved = partner_2(moved, "row", 0)
    moved = passed_along(moved, "row", -1)
    window_kv = join_partner(col_pair, moved, 2, row_odd)
    offsets = jnp.arange(2 * half_size, dtype=jnp.int32)
    key_rows = (
        row_id + row_odd - 1 + offsets // half_size
    ) % row_count * half_size + offsets % half_size
    key_cols = (
        col_id + col_odd - 1 + offsets // half_size
    ) % col_count * half_size + offsets % half_size
    valid_keys = (key_rows < row_count * half_size - pad_rows[0])[:, None] & (
        key_cols < col_count * half_size - pad_cols[0]
    )[None, :]
    pair_ids = jnp.arange(2, dtype=jnp.int32)
    row_tiles = (row_id + row_odd - 1 + pair_ids) % row_count
    col_tiles = (col_id + col_odd - 1 + pair_ids) % col_count
    key_labels = tile_labels(labels, row_tiles, col_tiles)
    key_labels = jnp.repeat(jnp.repeat(key_labels, half_size, axis=1), half_size, axis=2)
    own_labels = tile_labels(labels, jnp.reshape(row_id, (1,)), jnp.reshape(col_id, (1,)))
    query_labels = jnp.broadcast_to(own_labels, (frames, half_size, tile_cols)).reshape(-1)
    valid_tokens = jnp.broadcast_to(valid_keys[None], key_labels.shape).reshape(-1)
    allowed = (query_labels[:, None] == key_labels.reshape(-1)[None, :]) & valid_tokens[None, :]
    heads_here = channels // HDIM

    def split_heads(source):
        return source.reshape(-1, heads_here, HDIM).transpose(1, 0, 2)

    def one_head(operands):
        query_head, key_head, value_head = operands
        scores = jnp.einsum(
            "qd,kd->qk", query_head, key_head, preferred_element_type=jnp.float32
        ) * HDIM ** (-0.5)
        scores = jnp.where(allowed, scores, -1e30)
        row_max = jnp.max(scores, axis=1, keepdims=True)
        exponent = jnp.exp(scores - row_max)
        weights = (exponent / jnp.sum(exponent, axis=1, keepdims=True)).astype(jnp.bfloat16)
        return jnp.dot(weights, value_head, preferred_element_type=jnp.float32).astype(jnp.bfloat16)

    outputs = lax.map(
        one_head, (split_heads(queries), split_heads(window_kv[0]), split_heads(window_kv[1]))
    )
    return outputs.transpose(1, 0, 2).reshape(queries.shape)


def solution(mesh):
    placed = (
        P("grp", "row", "col", "hd"),
        P("grp", "row", "col", "hd"),
        P("grp", "row", "col", "hd"),
        P("grp", None, None),
        P("grp"),
        P("grp"),
    )
    return jax.shard_map(
        per_device,
        mesh=mesh,
        in_specs=placed,
        out_specs=P("grp", "row", "col", "hd"),
        check_vma=False,
    )
```

profile of v0, /device:TPU:8, one launch (start us, length us, event | category | flops | bytes accessed | tf_op | source)
XLA Modules:
  0.0 803.5 jit_solution(8355561080768716601)
XLA Ops:
  3.9 68.3 %collective-permute-done = bf16[2,4,16,16,768]{4,3,2,1,0:T(8,128)(2,1)S(1)} collective-permute-done((bf16[2,4,16,16,768]{4,3,2,1,0:T(8,128)(2,1)S(1)}, bf16[2,4,16,16,768]{4,3,2,1,0:T(8,128)(2,1)S(1)}, u32[]{:S(2)}, u32[]{:S(2)}) %collective-permute-start) | collective-permute-done | bytes 3145760 | tf_op jit(solution)/shard_map/ppermute | solution.py:11
  73.7 67.6 %collective-permute-done.1 = bf16[2,4,16,16,768]{4,3,2,1,0:T(8,128)(2,1)} collective-permute-done((bf16[2,4,16,16,768]{4,3,2,1,0:T(8,128)(2,1)S(1)}, bf16[2,4,16,16,768]{4,3,2,1,0:T(8,128)(2,1)}, u32[]{:S(2)}, u32[]{:S(2)}) %collective-permute-start.1) | collective-permute-done | bytes 3145760 | tf_op jit(solution)/shard_map/ppermute | solution.py:15
  142.8 66.9 %collective-permute-done.2 = bf16[2,4,16,16,768]{4,3,2,1,0:T(8,128)(2,1)} collective-permute-done((bf16[2,4,16,16,768]{4,3,2,1,0:T(8,128)(2,1)}, bf16[2,4,16,16,768]{4,3,2,1,0:T(8,128)(2,1)}, u32[]{:S(2)}, u32[]{:S(2)}) %collective-permute-start.2) | collective-permute-done | bytes 3145760 | tf_op jit(solution)/shard_map/ppermute | solution.py:11
  209.7 4.9 maximum_select_fusion.1
  218.8 133.0 %collective-permute-done.3 = bf16[2,4,16,32,768]{4,3,2,1,0:T(8,128)(2,1)S(1)} collective-permute-done((bf16[2,4,16,32,768]{4,3,2,1,0:T(8,128)(2,1)S(1)}, bf16[2,4,16,32,768]{4,3,2,1,0:T(8,128)(2,1)S(1)}, u32[]{:S(2)}, u32[]{:S(2)}) %collective-permute-start.3) | collective-permute-done | bytes 6291488 | tf_op jit(solution)/shard_map/ppermute | solution.py:11
  356.4 132.9 %collective-permute-done.4 = bf16[2,4,16,32,768]{4,3,2,1,0:T(8,128)(2,1)} collective-permute-done((bf16[2,4,16,32,768]{4,3,2,1,0:T(8,128)(2,1)S(1)}, bf16[2,4,16,32,768]{4,3,2,1,0:T(8,128)(2,1)}, u32[]{:S(2)}, u32[]{:S(2)}) %collective-permute-start.4) | collective-permute-done | bytes 6291488 | tf_op jit(solution)/shard_map/ppermute | solution.py:15
  499.5 122.9 %collective-permute-done.5 = bf16[2,4,16,32,768]{4,3,2,1,0:T(8,128)(2,1)} collective-permute-done((bf16[2,4,16,32,768]{4,3,2,1,0:T(8,128)(2,1)}, bf16[2,4,16,32,768]{4,3,2,1,0:T(8,128)(2,1)}, u32[]{:S(2)}, u32[]{:S(2)}) %collective-permute-start.5) | collective-permute-done | bytes 6291488 | tf_op jit(solution)/shard_map/ppermute | solution.py:11
  622.4 10.4 %maximum_select_fusion = bf16[2,4,32,32,768]{4,3,2,1,0:T(8,128)(2,1)S(1)} fusion(bf16[2,4,16,32,768]{4,3,2,1,0:T(8,128)(2,1)} %collective-permute-done.5, bf16[2,4,16,32,768]{4,3,2,1,0:T(8,128)(2,1)} %copy-done, pred[]{:T(512)S(6)} %eq.96), kind=kLoop, calls=%fused_computation.21 | loop fusion | flops 18874368 | bytes 25165824 | tf_op jit(solution)/shard_map/jit(_where)/select_n | solution.py:21
  632.7 5.4 fusion.29
  638.1 13.7 %reshape_squeeze.6 = bf16[4096,6,128]{2,1,0:T(8,128)(2,1)} reshape(bf16[1,4,32,32,768]{4,3,2,1,0:T(8,128)(2,1)} %get-tuple-element.102) | data formatting | bytes 12582912 | tf_op jit(solution)/shard_map/reshape;squeeze | solution.py:74
  651.8 6.9 copy.24
  658.7 13.7 %reshape_squeeze.7 = bf16[4096,6,128]{2,1,0:T(8,128)(2,1)} reshape(bf16[1,4,32,32,768]{4,3,2,1,0:T(8,128)(2,1)} %get-tuple-element.101) | data formatting | bytes 12582912 | tf_op jit(solution)/shard_map/reshape;squeeze | solution.py:74
  672.4 6.9 copy.25
  679.2 117.9 %while.11 = (s32[]{:T(128)}, bf16[6,1024,128]{2,1,0:T(8,128)(2,1)S(1)}, bf16[6,1024,128]{2,1,0:T(8,128)(2,1)}, bf16[6,4096,128]{2,1,0:T(8,128)(2,1)}, bf16[6,409...) while((s32[]{:T(128)}, ...), condition=%wide.region_7.8_spmd.clone, body=%wide.region_4.7_spmd.clone.sunk | while | flops 2223110144 | bytes 53049436 | solution.py:87
  679.2 5.9 fusion.35
  685.1 6.4 fusion.36
  691.5 7.3 fusion.37
  698.9 5.9 fusion.35
  704.8 6.4 fusion.36
  711.2 7.3 fusion.37
  718.5 5.9 fusion.35
  724.4 6.4 fusion.36
  730.8 7.3 fusion.37
  738.2 5.9 fusion.35
  744.1 6.4 fusion.36
  750.5 7.3 fusion.37
  757.8 5.9 fusion.35
  763.7 6.4 fusion.36
  770.1 7.3 fusion.37
  777.5 5.9 fusion.35
  783.4 6.4 fusion.36
  789.8 7.3 fusion.37
  (45 shorter events, 30.9 us)
Async XLA Ops:
  0.0 209.7 %copy-start.2 = (bf16[4,16,16,768]{3,2,1,0:T(8,128)(2,1)S(1)}, bf16[4,16,16,768]{3,2,1,0:T(8,128)(2,1)}, u32[]{:S(2)}) copy-start(bf16[4,16,16,768]{3,2,1,0:T(8,128)(2,1)} %param.9) | copy-start | bytes 4718596
  0.0 209.7 %copy-start.1 = (bf16[4,16,16,768]{3,2,1,0:T(8,128)(2,1)S(1)}, bf16[4,16,16,768]{3,2,1,0:T(8,128)(2,1)}, u32[]{:S(2)}) copy-start(bf16[4,16,16,768]{3,2,1,0:T(8,128)(2,1)} %param.10) | copy-start | bytes 4718596
  2.3 69.9 %collective-permute-start = (bf16[2,4,16,16,768]{4,3,2,1,0:T(8,128)(2,1)S(1)}, bf16[2,4,16,16,768]{4,3,2,1,0:T(8,128)(2,1)S(1)}, u32[]{:S(2)}, u32[]{:S(2)}) collective-permute-start(bf16[2,4,16,16,768]{4,3,2,1,0:T(8,128)(2,1)S(1)} %pad_maximum_fusion), channel_id=1, source_target_pairs={{0,2},{2,0},{1,3},{3,1},{4,6},{6,4},{5,7},{7,5},{8,10},{10,8},{9,1... | collective-permute-start | bytes 9437192 | tf_op jit(solution)/shard_map/ppermute | solution.py:11
  72.2 69.1 %collective-permute-start.1 = (bf16[2,4,16,16,768]{4,3,2,1,0:T(8,128)(2,1)S(1)}, bf16[2,4,16,16,768]{4,3,2,1,0:T(8,128)(2,1)}, u32[]{:S(2)}, u32[]{:S(2)}) collective-permute-start(bf16[2,4,16,16,768]{4,3,2,1,0:T(8,128)(2,1)S(1)} %collective-permute-done), channel_id=1, source_target_pairs={{0,2},{2,0},{1,3},{3,1},{4,6},{6,4},{5,7},{7,5},{8,10},{10,8},{9,1... | collective-permute-start | bytes 9437192 | tf_op jit(solution)/shard_map/ppermute | solution.py:15
  141.3 68.4 %collective-permute-start.2 = (bf16[2,4,16,16,768]{4,3,2,1,0:T(8,128)(2,1)}, bf16[2,4,16,16,768]{4,3,2,1,0:T(8,128)(2,1)}, u32[]{:S(2)}, u32[]{:S(2)}) collective-permute-start(bf16[2,4,16,16,768]{4,3,2,1,0:T(8,128)(2,1)} %collective-permute-done.1), channel_id=1, source_target_pairs={{0,2},{2,0},{1,3},{3,1},{4,6},{6,4},{5,7},{7,5},{8,10},{10,8},{9,1... | collective-permute-start | bytes 9437192 | tf_op jit(solution)/shard_map/ppermute | solution.py:11
  142.8 349.0 %copy-start.5 = (s32[4,4,2]{1,2,0:T(2,128)S(1)}, s32[4,4,2]{1,2,0:T(2,128)}, u32[]{:S(2)}) copy-start(s32[4,4,2]{1,2,0:T(2,128)} %param.11) | copy-start | bytes 388
  214.6 2.7 copy-start
  217.2 134.5 %collective-permute-start.3 = (bf16[2,4,16,32,768]{4,3,2,1,0:T(8,128)(2,1)S(1)}, bf16[2,4,16,32,768]{4,3,2,1,0:T(8,128)(2,1)S(1)}, u32[]{:S(2)}, u32[]{:S(2)}) collective-permute-start(bf16[2,4,16,32,768]{4,3,2,1,0:T(8,128)(2,1)S(1)} %maximum_select_fusion.1), channel_id=1, source_target_pairs={{0,4},{4,8},{8,12},{12,0},{1,5},{5,9},{9,13},{13,1},{2,6},{6,10},{... | collective-permute-start | bytes 18874376 | tf_op jit(solution)/shard_map/ppermute | solution.py:11
  351.8 137.5 %collective-permute-start.4 = (bf16[2,4,16,32,768]{4,3,2,1,0:T(8,128)(2,1)S(1)}, bf16[2,4,16,32,768]{4,3,2,1,0:T(8,128)(2,1)}, u32[]{:S(2)}, u32[]{:S(2)}) collective-permute-start(bf16[2,4,16,32,768]{4,3,2,1,0:T(8,128)(2,1)S(1)} %collective-permute-done.3), channel_id=1, source_target_pairs={{0,4},{4,0},{8,12},{12,8},{1,5},{5,1},{9,13},{13,9},{2,6},{6,2},{1... | collective-permute-start | bytes 18874376 | tf_op jit(solution)/shard_map/ppermute | solution.py:15
  489.2 133.1 %collective-permute-start.5 = (bf16[2,4,16,32,768]{4,3,2,1,0:T(8,128)(2,1)}, bf16[2,4,16,32,768]{4,3,2,1,0:T(8,128)(2,1)}, u32[]{:S(2)}, u32[]{:S(2)}) collective-permute-start(bf16[2,4,16,32,768]{4,3,2,1,0:T(8,128)(2,1)} %collective-permute-done.4), channel_id=1, source_target_pairs={{0,12},{4,0},{8,4},{12,8},{1,13},{5,1},{9,5},{13,9},{2,14},{6,2},{... | collective-permute-start | bytes 18874376 | tf_op jit(solution)/shard_map/ppermute | solution.py:11
  672.4 6.9 copy-start.3
  797.1 1.1 copy-start.4
where the time goes:
time: 808 us; the launch traced here: 803 us
  waiting for transfers between devices  592 us (73%)
  matrix products  79.3 us (10%)
  local copies, waits for them, and re-layouts  61 us (8%)
  other arithmetic  56.8 us (7%)
  starting transfers between devices  13.3 us (2%)
    ppermute x4, waiting for transfers between devices, passed_along(): lax.ppermute(value, axis, [(i, (i + by) % devices) for i in range(devices)])  391 us
    ppermute x2, waiting for transfers between devices, partner_2(): lax.ppermute(value, axis, [(i, i ^ 1 << apart) for i in range(lax.axis_si...  200 us
    dot_general x6, matrix products, one_head(): jnp.dot(weights, value_head, preferred_element_type=jnp.float32)  44 us
    reduce_sum x6, other arithmetic, one_head(): jnp.sum(exponent, axis=1, keepdims=True)  38.5 us
    dot_general x6, matrix products, one_head(): jnp.einsum('qd,kd->qk', query_head, key_head, preferred_element_type=jnp....  35.2 us
    another operation x2, local copies, waits for them, and re-layouts, split_heads(): return source.reshape(-1, heads_here, HDIM).transpose(1, 0, 2)  27.4 us
    unnamed x16, local copies, waits for them, and re-layouts  19 us
  transfers between devices with their start and end apart: 6, of which 6 were waited for; matrix products, arithmetic and copies ran while one was open for 1% of the time, Pallas kernels for 0%

commit v1 on v0

v1 whole, which is shorter than its diff:
```python
import functools
import math

import jax
import jax.numpy as jnp
from jax import lax
from jax.experimental import pallas as pl
from jax.experimental.pallas import tpu as pltpu
from jax.sharding import PartitionSpec as P

HDIM = 128
MESH = pl.DeviceIdType.MESH
MASKED = -1e30
SCALE = HDIM ** -0.5 * math.log2(math.e)
OWN, ROWS, COLS, DIAG = 0, 1, 2, 3
AHEAD = 2


def kernel(
    grid, sizes,
    q_hbm, k_hbm, v_hbm, labels, pad_rows, pad_cols, out_ref,
    q_buf, own, from_row, from_col, from_diag, bias, acc, top, total,
    local_sem, row_send, row_recv, col_send, col_recv, fwd_send, diag_recv,
):
    frames, half, width = grid
    n_row, n_col = sizes
    heads, tokens, _ = q_buf.shape
    block = half * width
    row = lax.axis_index("row")
    col = lax.axis_index("col")
    row2 = lax.rem(row + 2 * lax.rem(row, 2) - 1 + n_row, n_row)
    col2 = lax.rem(col + 2 * lax.rem(col, 2) - 1 + n_col, n_col)

    barrier = pltpu.get_barrier_semaphore()
    pl.semaphore_signal(barrier, inc=1, device_id={"row": row2}, device_id_type=MESH)
    pl.semaphore_signal(barrier, inc=1, device_id={"col": col2}, device_id_type=MESH)

    def lanes(h):
        return pl.ds(pl.multiple_of(h * HDIM, HDIM), HDIM)

    def local(h):
        sources = (k_hbm, v_hbm, q_hbm)
        targets = (own.at[0, h], own.at[1, h], q_buf.at[h])
        return [
            pltpu.make_async_copy(s.at[:, lanes(h)], t, local_sem.at[i, h])
            for i, (s, t) in enumerate(zip(sources, targets))
        ]

    def to_row(h):
        return [
            pltpu.make_async_remote_copy(
                s.at[:, lanes(h)], from_row.at[i, h], row_send.at[i, h], row_recv.at[i, h],
                device_id={"row": row2}, device_id_type=MESH)
            for i, s in enumerate((k_hbm, v_hbm))
        ]

    def to_col(h):
        return [
            pltpu.make_async_remote_copy(
                s.at[:, lanes(h)], from_col.at[i, h], col_send.at[i, h], col_recv.at[i, h],
                device_id={"col": col2}, device_id_type=MESH)
            for i, s in enumerate((k_hbm, v_hbm))
        ]

    def forward(h):
        return [
            pltpu.make_async_remote_copy(
                from_row.at[i, h], from_diag.at[i, h], fwd_send.at[i, h], diag_recv.at[i, h],
                device_id={"col": col2}, device_id_type=MESH)
            for i in range(2)
        ]

    def each(count, do):
        lax.fori_loop(0, count, lambda h, c: (do(h), c)[1], 0)

    def start_all(make):
        def do(h):
            for copy in make(h):
                copy.start()
        return do

    each(heads, start_all(local))
    pl.semaphore_wait(barrier, 2)
    each(AHEAD, start_all(lambda h: to_row(h) + to_col(h)))
    lax.fori_loop(AHEAD, heads, lambda h, c: (start_all(to_row)(h), c)[1], 0)

    token = lax.broadcasted_iota(jnp.int32, (1, tokens), 1)
    token_frame = token // block
    token_row = token % block // width
    token_col = token % width
    for slot, (r, c) in enumerate(((row, col), (row2, col), (row, col2), (row2, col2))):
        valid = (r * half + token_row < n_row * half - pad_rows[0]) & (
            c * width + token_col < n_col * width - pad_cols[0])
        key_label = jnp.full((1, tokens), labels[0, r, c], jnp.int32)
        for f in range(1, frames):
            key_label = jnp.where(token_frame == f, labels[f, r, c], key_label)
        for f in range(frames):
            allowed = valid & (key_label == labels[f, row, col])
            bias[pl.ds(slot * frames + f, 1), :] = jnp.where(allowed, 0.0, MASKED)

    def unit(slot, h, tile):
        k = tile[0, h]
        v = tile[1, h]
        for f in range(frames):
            rows = pl.ds(f * block, block)
            s = lax.dot_general(
                q_buf[h, rows, :], k, (((1,), (1,)), ((), ())),
                preferred_element_type=jnp.float32)
            s = s * SCALE + bias[pl.ds(slot * frames + f, 1), :]
            high = jnp.max(s, axis=1, keepdims=True)
            if slot != OWN:
                before = top[h, rows, :]
                high = jnp.maximum(high, before)
            p = jnp.exp2(s - high)
            sums = jnp.sum(p, axis=1, keepdims=True)
            part = jnp.dot(p.astype(jnp.bfloat16), v, preferred_element_type=jnp.float32)
            if slot != OWN:
                shrink = jnp.exp2(before - high)
                sums = sums + shrink * total[h, rows, :]
                part = part + shrink * acc[h, rows, :]
            if slot == DIAG:
                out_ref[rows, lanes(h)] = (part / sums).astype(out_ref.dtype)
            else:
                top[h, rows, :] = high
                total[h, rows, :] = sums
                acc[h, rows, :] = part

    def finish(h):
        for copy in forward(h):
            copy.wait_recv()
        unit(DIAG, h, from_diag)

    def step(h):
        for copy in local(h):
            copy.wait()
        unit(OWN, h, own)
        for arrived, onward in zip(to_row(h), forward(h)):
            arrived.wait_recv()
            onward.start()

        @pl.when(h + AHEAD < heads)
        def _():
            start_all(to_col)(h + AHEAD)

        unit(ROWS, h, from_row)
        for copy in to_col(h):
            copy.wait_recv()
        unit(COLS, h, from_col)

        @pl.when(h > 0)
        def _():
            finish(h - 1)

    each(heads, step)
    finish(heads - 1)

    def drain(h):
        for copy in to_row(h) + to_col(h) + forward(h):
            copy.wait_send()

    each(heads, drain)


def per_device(sizes, queries, keys, values, labels, pad_rows, pad_cols):
    frames, half, width, channels = queries.shape
    heads = channels // HDIM
    tokens = frames * half * width
    flat = (tokens, channels)
    tile = pltpu.VMEM((2, heads, tokens, HDIM), jnp.bfloat16)
    any_space = pl.BlockSpec(memory_space=pl.ANY)
    smem = pl.BlockSpec(memory_space=pltpu.SMEM)
    copies = pltpu.SemaphoreType.DMA((2, heads))
    out = pl.pallas_call(
        functools.partial(kernel, (frames, half, width), sizes),
        out_shape=jax.ShapeDtypeStruct(flat, queries.dtype),
        in_specs=[any_space] * 3 + [smem] * 3,
        out_specs=pl.BlockSpec(memory_space=pltpu.VMEM),
        scratch_shapes=[
            pltpu.VMEM((heads, tokens, HDIM), jnp.bfloat16),
            tile, tile, tile, tile,
            pltpu.VMEM((4 * frames, tokens), jnp.float32),
            pltpu.VMEM((heads, tokens, HDIM), jnp.float32),
            pltpu.VMEM((heads, tokens, 1), jnp.float32),
            pltpu.VMEM((heads, tokens, 1), jnp.float32),
            pltpu.SemaphoreType.DMA((3, heads)),
            copies, copies, copies, copies, copies, copies,
        ],
        compiler_params=pltpu.CompilerParams(
            collective_id=0, has_side_effects=True, vmem_limit_bytes=48 * 2 ** 20),
        cost_estimate=pl.CostEstimate(
            flops=16 * tokens * tokens * channels,
            bytes_accessed=8 * tokens * channels,
            transcendentals=4 * tokens * tokens * heads),
    )(queries.reshape(flat), keys.reshape(flat), values.reshape(flat), labels, pad_rows, pad_cols)
    return out.reshape(queries.shape)


def solution(mesh):
    placed = (
        P("grp", "row", "col", "hd"),
        P("grp", "row", "col", "hd"),
        P("grp", "row", "col", "hd"),
        P("grp", None, None),
        P("grp"),
        P("grp"),
    )
    return jax.shard_map(
        functools.partial(per_device, (mesh.shape["row"], mesh.shape["col"])),
        mesh=mesh,
        in_specs=placed,
        out_specs=P("grp", "row", "col", "hd"),
        check_vma=False,
    )
```

time: 808 us -> 200 us (0.25)
  waiting for transfers between devices: 592 us -> 0 us
  Pallas kernels: 0 us -> 194 us
  matrix products: 79.3 us -> 0 us
  other arithmetic: 56.8 us -> 0 us
  local copies, waits for them, and re-layouts: 61 us -> 4.75 us
  starting transfers between devices: 13.3 us -> 0 us
    ppermute x6 -> x0, waiting for transfers between devices: 592 us -> none  [the longest x4 391 us: passed_along(): lax.ppermute(value, axis, [(i, (i + by) % devices) for i in range(devices)])]
    pallas_call x0 -> x1, Pallas kernels: none -> 194 us  [per_device(): pl.pallas_call(functools.partial(kernel, (frames, half, width), sizes), o...]
    dot_general x12 -> x0, matrix products: 79.3 us -> none  [the longest x6 44 us: one_head(): jnp.dot(weights, value_head, preferred_element_type=jnp.float32)]
    reduce_sum x10 -> x0, other arithmetic: 39 us -> none  [the longest x6 38.5 us: one_head(): jnp.sum(exponent, axis=1, keepdims=True)]
    another operation x2 -> x0, local copies, waits for them, and re-layouts: 27.4 us -> none  [split_heads(): return source.reshape(-1, heads_here, HDIM).transpose(1, 0, 2)]
    select_n x4 -> x0, other arithmetic: 15.3 us -> none  [the longest x2 15.2 us: join_partner(): return jnp.where(odd_flag == 1, with_upper, with_lower)]
    unnamed x16 -> x6, local copies, waits for them, and re-layouts: 19 us -> 4.75 us
    ppermute x6 -> x0, starting transfers between devices: 13.3 us -> none  [the longest x4 7.21 us: passed_along(): lax.ppermute(value, axis, [(i, (i + by) % devices) for i in range(devices)])]
  transfers between devices with their start and end apart: 6 -> 0, of which waited for: 6 -> 0; matrix products, arithmetic and copies ran while one was open for 1% -> 0% of each run, Pallas kernels for 0% -> 0%
where the time goes in v1:
time: 200 us
  Pallas kernels  194 us (97%)
  local copies, waits for them, and re-layouts  4.75 us (2%)
    pallas_call x1, Pallas kernels, per_device(): pl.pallas_call(functools.partial(kernel, (frames, half, width), sizes), o...  194 us
    unnamed x6, local copies, waits for them, and re-layouts  4.75 us

profile of v1, /device:TPU:8, one launch (start us, length us, event | category | flops | bytes accessed | tf_op | source)
XLA Modules:
  0.0 200.1 jit_solution(5971221627909010877)
XLA Ops:
  1.3 0.8 copy.7.labels
  2.1 0.0 copy-start
  2.1 1.4 copy-done
  3.5 0.0 copy-start.1
  3.5 1.4 copy-done.1
  4.9 194.0 %shard_map.64 = bf16[1024,768]{1,0:T(8,128)(2,1)S(1)} custom-call(bf16[1024,768]{1,0:T(8,128)(2,1)S(1)} %bitcast.5, bf16[1024,768]{1,0:T(8,128)(2,1)S(1)} %bitcast.6, bf16[1024,768]{1,0:T(8,128)(2,1)} %bitcast.7, s32[4,4,2]{2,1,0:T(4,128)S(1)} %copy.7.labels, s32[1]{0:T(128)S(6)} %copy.9.pad_rows, s32[1]{0:T(128)S(6)} %copy.10.pad_cols), custom_call_target="tpu_custom_call" | custom-call | flops 12884901888 | bytes 6291456 | tf_op jit(solution)/shard_map/pallas_call | solution.py:173
  198.9 1.1 copy.11
Async XLA Ops:
  2.1 1.4 copy-start
  3.5 1.4 copy-start.1

commit v2 on v1

--- a/solution.py
+++ b/solution.py
@@ -13,7 +13,7 @@
 MASKED = -1e30
 SCALE = HDIM ** -0.5 * math.log2(math.e)
 OWN, ROWS, COLS, DIAG = 0, 1, 2, 3
-AHEAD = 2
+LAG = 2
 
 
 def kernel(
@@ -81,8 +81,7 @@
 
     each(heads, start_all(local))
     pl.semaphore_wait(barrier, 2)
-    each(AHEAD, start_all(lambda h: to_row(h) + to_col(h)))
-    lax.fori_loop(AHEAD, heads, lambda h, c: (start_all(to_row)(h), c)[1], 0)
+    each(heads, start_all(lambda h: to_row(h) + to_col(h)))
 
     token = lax.broadcasted_iota(jnp.int32, (1, tokens), 1)
     token_frame = token // block
@@ -130,29 +129,38 @@
             copy.wait_recv()
         unit(DIAG, h, from_diag)
 
-    def step(h):
+    def near(h):
         for copy in local(h):
             copy.wait()
         unit(OWN, h, own)
+
+        @pl.when(h > 0)
+        def _():
+            column(h - 1)
+
+    def column(h):
+        for copy in to_col(h):
+            copy.wait_recv()
+        unit(COLS, h, from_col)
+
+    def far(h):
         for arrived, onward in zip(to_row(h), forward(h)):
             arrived.wait_recv()
             onward.start()
 
-        @pl.when(h + AHEAD < heads)
+        @pl.when(h == 0)
         def _():
-            start_all(to_col)(h + AHEAD)
+            column(heads - 1)
 
         unit(ROWS, h, from_row)
-        for copy in to_col(h):
-            copy.wait_recv()
-        unit(COLS, h, from_col)
-
-        @pl.when(h > 0)
+
+        @pl.when(h >= LAG)
         def _():
-            finish(h - 1)
-
-    each(heads, step)
-    finish(heads - 1)
+            finish(h - LAG)
+
+    each(heads, near)
+    each(heads, far)
+    lax.fori_loop(heads - LAG, heads, lambda h, c: (finish(h), c)[1], 0)
 
     def drain(h):
         for copy in to_row(h) + to_col(h) + forward(h):
@@ -186,7 +194,7 @@
             copies, copies, copies, copies, copies, copies,
         ],
         compiler_params=pltpu.CompilerParams(
-            collective_id=0, has_side_effects=True, vmem_limit_bytes=48 * 2 ** 20),
+            collective_id=0, has_side_effects=True, vmem_limit_bytes=60 * 2 ** 20),
         cost_estimate=pl.CostEstimate(
             flops=16 * tokens * tokens * channels,
             bytes_accessed=8 * tokens * channels,

time: 200 us -> 157 us (0.79)
  Pallas kernels: 194 us -> 152 us
    pallas_call x1, Pallas kernels: 194 us -> 152 us  [per_device(): pl.pallas_call(functools.partial(kernel, (frames, half, width), sizes), o...]
    unnamed x6 -> x2, local copies, waits for them, and re-layouts: 4.75 us -> 4.05 us
where the time goes in v2:
time: 157 us
  Pallas kernels  152 us (97%)
  local copies, waits for them, and re-layouts  4.05 us (3%)
    pallas_call x1, Pallas kernels, per_device(): pl.pallas_call(functools.partial(kernel, (frames, half, width), sizes), o...  152 us
    unnamed x2, local copies, waits for them, and re-layouts  4.05 us

profile of v2, /device:TPU:8, one launch (start us, length us, event | category | flops | bytes accessed | tf_op | source)
XLA Modules:
  0.0 157.2 jit_solution(17858081298481273158)
XLA Ops:
  1.3 1.4 copy.7.labels
  2.7 151.9 %shard_map.64 = bf16[1024,768]{1,0:T(8,128)(2,1)} custom-call(bf16[1024,768]{1,0:T(8,128)(2,1)} %bitcast.5, bf16[1024,768]{1,0:T(8,128)(2,1)} %bitcast.6, bf16[1024,768]{1,0:T(8,128)(2,1)} %bitcast.7, s32[4,4,2]{2,1,0:T(4,128)} %copy.7.labels, s32[1]{0:T(128)S(6)} %copy.9.pad_rows, s32[1]{0:T(128)S(6)} %copy.10.pad_cols), custom_call_target="tpu_custom_call" | custom-call | flops 12884901888 | bytes 6291456 | tf_op jit(solution)/shard_map/pallas_call | solution.py:181
  154.6 2.7 %copy.11 = bf16[4,16,16,768]{3,2,1,0:T(8,128)(2,1)} copy(bf16[4,16,16,768]{3,2,1,0:T(8,128)(2,1)} %bitcast.4) | data formatting | bytes 3145728

commit v3 on v2

--- a/solution.py
+++ b/solution.py
@@ -13,19 +13,20 @@
 MASKED = -1e30
 SCALE = HDIM ** -0.5 * math.log2(math.e)
 OWN, ROWS, COLS, DIAG = 0, 1, 2, 3
-LAG = 2
+PARTS = 2
 
 
 def kernel(
     grid, sizes,
-    q_hbm, k_hbm, v_hbm, labels, pad_rows, pad_cols, out_ref,
-    q_buf, own, from_row, from_col, from_diag, bias, acc, top, total,
+    q_hbm, k_hbm, v_hbm, labels_hbm, pad_rows, pad_cols, out_ref,
+    q_buf, own, from_row, from_col, from_diag, bias, acc, top, total, labels, label_sem,
     local_sem, row_send, row_recv, col_send, col_recv, fwd_send, diag_recv,
 ):
     frames, half, width = grid
     n_row, n_col = sizes
     heads, tokens, _ = q_buf.shape
     block = half * width
+    size = tokens // PARTS
     row = lax.axis_index("row")
     col = lax.axis_index("col")
     row2 = lax.rem(row + 2 * lax.rem(row, 2) - 1 + n_row, n_row)
@@ -38,6 +39,14 @@
     def lanes(h):
         return pl.ds(pl.multiple_of(h * HDIM, HDIM), HDIM)
 
+    def piece(p):
+        if p is None:
+            return pl.ds(0, tokens)
+        return pl.ds(p * size, size)
+
+    def mark(p):
+        return 0 if p is None else p
+
     def local(h):
         sources = (k_hbm, v_hbm, q_hbm)
         targets = (own.at[0, h], own.at[1, h], q_buf.at[h])
@@ -46,10 +55,11 @@
             for i, (s, t) in enumerate(zip(sources, targets))
         ]
 
-    def to_row(h):
+    def to_row(h, p=None):
         return [
             pltpu.make_async_remote_copy(
-                s.at[:, lanes(h)], from_row.at[i, h], row_send.at[i, h], row_recv.at[i, h],
+                s.at[piece(p), lanes(h)], from_row.at[i, h, piece(p)],
+                row_send.at[i, h, mark(p)], row_recv.at[i, h, mark(p)],
                 device_id={"row": row2}, device_id_type=MESH)
             for i, s in enumerate((k_hbm, v_hbm))
         ]
@@ -62,10 +72,11 @@
             for i, s in enumerate((k_hbm, v_hbm))
         ]
 
-    def forward(h):
+    def forward(h, p=None):
         return [
             pltpu.make_async_remote_copy(
-                from_row.at[i, h], from_diag.at[i, h], fwd_send.at[i, h], diag_recv.at[i, h],
+                from_row.at[i, h, piece(p)], from_diag.at[i, h, piece(p)],
+                fwd_send.at[i, h, mark(p)], diag_recv.at[i, h, mark(p)],
                 device_id={"col": col2}, device_id_type=MESH)
             for i in range(2)
         ]
@@ -79,10 +90,18 @@
                 copy.start()
         return do
 
+    label_copy = pltpu.make_async_copy(labels_hbm, labels, label_sem)
+    label_copy.start()
     each(heads, start_all(local))
     pl.semaphore_wait(barrier, 2)
-    each(heads, start_all(lambda h: to_row(h) + to_col(h)))
-
+
+    last = heads - 1
+    each(last, start_all(lambda h: to_col(h) + to_row(h)))
+    for part in range(PARTS):
+        start_all(lambda h: to_row(h, part))(last)
+    start_all(to_col)(last)
+
+    label_copy.wait()
     token = lax.broadcasted_iota(jnp.int32, (1, tokens), 1)
     token_frame = token // block
     token_row = token % block // width
@@ -97,37 +116,47 @@
             allowed = valid & (key_label == labels[f, row, col])
             bias[pl.ds(slot * frames + f, 1), :] = jnp.where(allowed, 0.0, MASKED)
 
-    def unit(slot, h, tile):
-        k = tile[0, h]
-        v = tile[1, h]
+    def unit(slot, h, tile, part=None):
+        start, count = (0, tokens) if part is None else (part * size, size)
+        keys = pl.ds(start, count)
+        k = tile[0, h, keys, :]
+        v = tile[1, h, keys, :]
         for f in range(frames):
             rows = pl.ds(f * block, block)
             s = lax.dot_general(
                 q_buf[h, rows, :], k, (((1,), (1,)), ((), ())),
                 preferred_element_type=jnp.float32)
-            s = s * SCALE + bias[pl.ds(slot * frames + f, 1), :]
+            s = s * SCALE + bias[pl.ds(slot * frames + f, 1), keys]
             high = jnp.max(s, axis=1, keepdims=True)
             if slot != OWN:
                 before = top[h, rows, :]
                 high = jnp.maximum(high, before)
             p = jnp.exp2(s - high)
             sums = jnp.sum(p, axis=1, keepdims=True)
-            part = jnp.dot(p.astype(jnp.bfloat16), v, preferred_element_type=jnp.float32)
+            added = jnp.dot(p.astype(jnp.bfloat16), v, preferred_element_type=jnp.float32)
             if slot != OWN:
                 shrink = jnp.exp2(before - high)
                 sums = sums + shrink * total[h, rows, :]
-                part = part + shrink * acc[h, rows, :]
-            if slot == DIAG:
-                out_ref[rows, lanes(h)] = (part / sums).astype(out_ref.dtype)
+                added = added + shrink * acc[h, rows, :]
+            if slot == DIAG and part in (None, PARTS - 1):
+                out_ref[rows, lanes(h)] = (added / sums).astype(out_ref.dtype)
             else:
                 top[h, rows, :] = high
                 total[h, rows, :] = sums
-                acc[h, rows, :] = part
+                acc[h, rows, :] = added
+
+    def arrive(h, p=None):
+        for copy in forward(h, p):
+            copy.wait_recv()
 
     def finish(h):
-        for copy in forward(h):
-            copy.wait_recv()
+        arrive(h)
         unit(DIAG, h, from_diag)
+
+    def pass_on(h, p=None):
+        for arrived, onward in zip(to_row(h, p), forward(h, p)):
+            arrived.wait_recv()
+            onward.start()
 
     def near(h):
         for copy in local(h):
@@ -144,9 +173,11 @@
         unit(COLS, h, from_col)
 
     def far(h):
-        for arrived, onward in zip(to_row(h), forward(h)):
-            arrived.wait_recv()
-            onward.start()
+        @pl.when(h >= 2)
+        def _():
+            finish(h - 2)
+
+        pass_on(h)
 
         @pl.when(h == 0)
         def _():
@@ -154,19 +185,28 @@
 
         unit(ROWS, h, from_row)
 
-        @pl.when(h >= LAG)
-        def _():
-            finish(h - LAG)
-
     each(heads, near)
-    each(heads, far)
-    lax.fori_loop(heads - LAG, heads, lambda h, c: (finish(h), c)[1], 0)
+    each(last, far)
+    finish(last - 2)
+    for part in range(PARTS):
+        pass_on(last, part)
+        if part == 0:
+            finish(last - 1)
+        unit(ROWS, last, from_row, part)
+    for part in range(PARTS):
+        arrive(last, part)
+        unit(DIAG, last, from_diag, part)
 
     def drain(h):
-        for copy in to_row(h) + to_col(h) + forward(h):
+        for copy in to_row(h) + forward(h) + to_col(h):
             copy.wait_send()
 
-    each(heads, drain)
+    each(last, drain)
+    for part in range(PARTS):
+        for copy in to_row(last, part) + forward(last, part):
+            copy.wait_send()
+    for copy in to_col(last):
+        copy.wait_send()
 
 
 def per_device(sizes, queries, keys, values, labels, pad_rows, pad_cols):
@@ -175,13 +215,14 @@
     tokens = frames * half * width
     flat = (tokens, channels)
     tile = pltpu.VMEM((2, heads, tokens, HDIM), jnp.bfloat16)
-    any_space = pl.BlockSpec(memory_space=pl.ANY)
+    any_space = pl.BlockSpec(memory_space=pltpu.HBM)
     smem = pl.BlockSpec(memory_space=pltpu.SMEM)
     copies = pltpu.SemaphoreType.DMA((2, heads))
+    part_copies = pltpu.SemaphoreType.DMA((2, heads, PARTS))
     out = pl.pallas_call(
         functools.partial(kernel, (frames, half, width), sizes),
         out_shape=jax.ShapeDtypeStruct(flat, queries.dtype),
-        in_specs=[any_space] * 3 + [smem] * 3,
+        in_specs=[any_space] * 4 + [smem] * 2,
         out_specs=pl.BlockSpec(memory_space=pltpu.VMEM),
         scratch_shapes=[
             pltpu.VMEM((heads, tokens, HDIM), jnp.bfloat16),
@@ -190,11 +231,13 @@
             pltpu.VMEM((heads, tokens, HDIM), jnp.float32),
             pltpu.VMEM((heads, tokens, 1), jnp.float32),
             pltpu.VMEM((heads, tokens, 1), jnp.float32),
+            pltpu.SMEM(labels.shape, jnp.int32),
+            pltpu.SemaphoreType.DMA,
             pltpu.SemaphoreType.DMA((3, heads)),
-            copies, copies, copies, copies, copies, copies,
+            part_copies, part_copies, copies, copies, part_copies, part_copies,
         ],
         compiler_params=pltpu.CompilerParams(
-            collective_id=0, has_side_effects=True, vmem_limit_bytes=60 * 2 ** 20),
+            collective_id=0, has_side_effects=True, vmem_limit_bytes=48 * 2 ** 20),
         cost_estimate=pl.CostEstimate(
             flops=16 * tokens * tokens * channels,
             bytes_accessed=8 * tokens * channels,

time: 157 us -> 154 us (0.981)
  Pallas kernels: 152 us -> 148 us
    pallas_call x1, Pallas kernels: 152 us -> 148 us  [per_device(): pl.pallas_call(functools.partial(kernel, (frames, half, width), sizes), o...]
    unnamed x2 -> x6, local copies, waits for them, and re-layouts: 4.05 us -> 4.75 us
where the time goes in v3:
time: 154 us
  Pallas kernels  148 us (96%)
  local copies, waits for them, and re-layouts  4.75 us (3%)
    pallas_call x1, Pallas kernels, per_device(): pl.pallas_call(functools.partial(kernel, (frames, half, width), sizes), o...  148 us
    unnamed x6, local copies, waits for them, and re-layouts  4.75 us

profile of v3, /device:TPU:8, one launch (start us, length us, event | category | flops | bytes accessed | tf_op | source)
XLA Modules:
  0.0 154.0 jit_solution(8304669872722811386)
XLA Ops:
  1.3 0.8 copy.7.labels_hbm
  2.1 0.0 copy-start
  2.1 1.4 copy-done
  3.5 0.0 copy-start.1
  3.5 1.4 copy-done.1
  4.9 147.9 %shard_map.64 = bf16[1024,768]{1,0:T(8,128)(2,1)S(1)} custom-call(bf16[1024,768]{1,0:T(8,128)(2,1)S(1)} %bitcast.5, bf16[1024,768]{1,0:T(8,128)(2,1)S(1)} %bitcast.6, bf16[1024,768]{1,0:T(8,128)(2,1)} %bitcast.7, s32[4,4,2]{2,1,0:T(4,128)S(1)} %copy.7.labels_hbm, s32[1]{0:T(128)S(6)} %copy.9.pad_rows, s32[1]{0:T(128)S(6)} %copy.10.pad_cols), custom_call_target="tpu_custom_call" | custom-call | flops 12884901888 | bytes 6291456 | tf_op jit(solution)/shard_map/pallas_call | solution.py:222
  152.8 1.1 copy.11
Async XLA Ops:
  2.1 1.4 copy-start
  3.5 1.4 copy-start.1

commit v4 on v3

--- a/solution.py
+++ b/solution.py
@@ -237,7 +237,7 @@
             part_copies, part_copies, copies, copies, part_copies, part_copies,
         ],
         compiler_params=pltpu.CompilerParams(
-            collective_id=0, has_side_effects=True, vmem_limit_bytes=48 * 2 ** 20),
+            collective_id=0, has_side_effects=True, vmem_limit_bytes=52 * 2 ** 20),
         cost_estimate=pl.CostEstimate(
             flops=16 * tokens * tokens * channels,
             bytes_accessed=8 * tokens * channels,

time: 154 us -> 151 us (0.981)
  local copies, waits for them, and re-layouts: 4.75 us -> 1.94 us
    unnamed x6 -> x2, local copies, waits for them, and re-layouts: 4.75 us -> 1.94 us
where the time goes in v4:
time: 151 us
  Pallas kernels  148 us (98%)
  local copies, waits for them, and re-layouts  1.94 us (1%)
    pallas_call x1, Pallas kernels, per_device(): pl.pallas_call(functools.partial(kernel, (frames, half, width), sizes), o...  148 us

profile of v4, /device:TPU:8, one launch (start us, length us, event | category | flops | bytes accessed | tf_op | source)
XLA Modules:
  0.0 150.8 jit_solution(12628449046404326875)
XLA Ops:
  1.3 0.8 copy.7.labels_hbm
  2.1 147.5 %shard_map.64 = bf16[1024,768]{1,0:T(8,128)(2,1)S(1)} custom-call(bf16[1024,768]{1,0:T(8,128)(2,1)} %bitcast.5, bf16[1024,768]{1,0:T(8,128)(2,1)} %bitcast.6, bf16[1024,768]{1,0:T(8,128)(2,1)} %bitcast.7, s32[4,4,2]{2,1,0:T(4,128)S(1)} %copy.7.labels_hbm, s32[1]{0:T(128)S(6)} %copy.9.pad_rows, s32[1]{0:T(128)S(6)} %copy.10.pad_cols), custom_call_target="tpu_custom_call" | custom-call | flops 12884901888 | bytes 6291456 | tf_op jit(solution)/shard_map/pallas_call | solution.py:222
  149.6 1.1 copy.11
